TPU v7x, 32 devices: a whole 2x2x4 slice. The times are simulated.
32 devices in a mesh: ctx: 16 (over z, x, core), head: 2 (over y).
Axes of the slice: x: 2, y: 2, z: 4, core: 2. Of those that a mesh axis runs over, the one named last changes fastest.
Arguments:
- query_nope: bfloat16 [2048, 16384], P('ctx', 'head'), may hold values from -6 to 6
- query_rope: bfloat16 [2048, 8192], P('ctx', 'head'), may hold values from -80 to 80
- out_grad: bfloat16 [2048, 16384], P('ctx', 'head'), may hold values from -6 to 6
- latent_codes: bfloat16 [2048, 512], P('ctx'), may hold values from -4 to 4
- scale_exponents: int32 [2048, 4], P('ctx'), may hold values from -2 to 1
- key_rope: bfloat16 [2048, 64], P('ctx'), may hold values from -2 to 2
- block_order: int32 [16], P('ctx'), may hold values from 0 to 15, each once
- up_keys: bfloat16 [128, 512, 128], P('head'), may hold values from -0.25 to 0.25
- up_values: bfloat16 [128, 512, 128], P('head'), may hold values from -0.25 to 0.25
Outputs:
- grad_query_nope: bfloat16 [2048, 16384], P('ctx', 'head')
- grad_query_rope: bfloat16 [2048, 8192], P('ctx', 'head')
- grad_latent: float32 [2048, 512], P('ctx')
- grad_key_rope: float32 [2048, 64], P('ctx')
All inputs are finite; a program needn't handle non-finite values.
Results may differ from a plain program's by a relative error of at most 0.0097.
Values may be sent and summed in bfloat16 or wider, within the bound.
A program may use at most 192 MiB of HBM per device.

v0:
```python
import functools
import math

import jax
import jax.numpy as jnp
from jax import lax
from jax.experimental import pallas as pl
from jax.experimental.pallas import tpu as pltpu
from jax.sharding import PartitionSpec as P

STEPS = 4
F32 = jnp.float32
BF16 = jnp.bfloat16


def shifted(block, axis, distance):
    devices = range(lax.axis_size(axis))
    route = [((i - distance) % len(devices), i) for i in devices]
    return lax.ppermute(block, axis, route)


def nt(a, b):
    return lax.dot_general(a, b, (((1,), (1,)), ((), ())), preferred_element_type=F32)


def nn(a, b):
    return lax.dot_general(a, b, (((1,), (0,)), ((), ())), preferred_element_type=F32)


def tn(a, b):
    return lax.dot_general(a, b, (((0,), (0,)), ((), ())), preferred_element_type=F32)


def attend(
    dims,
    pack0,
    pack1,
    pack2,
    pack3,
    q_ref,
    qr_ref,
    g_ref,
    uk_ref,
    uv_ref,
    dq_ref,
    dqr_ref,
    dlat_ref,
    drope_ref,
    lat,
    rope_even,
    rope_odd,
    bias,
):
    tokens, width, nope, rope, group = dims
    step = pl.program_id(0)
    factor = 1.0 / math.sqrt(nope + rope)
    log2_scale = factor * math.log2(math.e)

    @pl.when(step == 0)
    def _():
        lane = lax.broadcasted_iota(jnp.int32, (tokens, 2 * rope), 1)
        row = lax.broadcasted_iota(jnp.int32, (tokens, tokens), 0).astype(F32)
        col = lax.broadcasted_iota(jnp.int32, (tokens, tokens), 1).astype(F32)
        own = None
        for s, pack in enumerate((pack0, pack1, pack2, pack3)):
            rows = pl.ds(s * tokens, tokens)
            lat[rows, :] = pack[:, :width]
            tail = pack[:, width:].astype(F32)
            turned = pltpu.roll(tail, rope, 1)
            rope_even[rows, :] = jnp.where(lane < rope, tail, 0.0).astype(BF16)
            rope_odd[rows, :] = jnp.where(lane >= rope, turned, 0.0).astype(BF16)
            place = jnp.broadcast_to(tail[:, rope : rope + 1], (tokens, tokens)) * tokens
            if s == 0:
                own = place
            bias[rows, :] = jnp.where(place + row <= own + col, 0.0, -jnp.inf)
        dlat_ref[...] = jnp.zeros_like(dlat_ref)
        drope_ref[...] = jnp.zeros_like(drope_ref)

    latent = lat[...]
    lane_q = lax.broadcasted_iota(jnp.int32, (tokens, 2 * rope), 1)
    for pair in range(group // 2):
        first, second = 2 * pair, 2 * pair + 1
        qr = qr_ref[:, pair * 2 * rope : (pair + 1) * 2 * rope]
        keys = nn(latent, jnp.concatenate([uk_ref[first], uk_ref[second]], axis=1)).astype(BF16)
        q = [q_ref[:, h * nope : (h + 1) * nope] for h in (first, second)]
        g = [g_ref[:, h * nope : (h + 1) * nope] for h in (first, second)]
        q_lat = [(nt(q[i], uk_ref[h]) * factor).astype(BF16) for i, h in enumerate((first, second))]
        g_lat = [nt(g[i], uv_ref[h]).astype(BF16) for i, h in enumerate((first, second))]
        dp_both = nt(latent, jnp.concatenate(g_lat, axis=0))
        left = []
        right = []
        turned = None
        scores = []
        for i in range(2):
            full_keys = jnp.concatenate(
                [keys[:, i * nope : (i + 1) * nope], (rope_even, rope_odd)[i][...]], axis=1
            )
            raw = nt(full_keys, jnp.concatenate([q[i], qr], axis=1))
            score = raw * log2_scale + bias[...]
            top = jnp.max(score, axis=0, keepdims=True)
            weight = jnp.exp2(score - top)
            inverse = 1.0 / jnp.sum(weight, axis=0, keepdims=True)
            dp = dp_both[:, i * tokens : (i + 1) * tokens]
            delta = jnp.sum(weight * dp, axis=0, keepdims=True) * inverse
            prob = weight * inverse
            ds = (prob * (dp - delta)).astype(BF16)
            scores.append(ds)
            left += [ds, prob.astype(BF16)]
            right += [q_lat[i], g_lat[i]]
            grad = tn(ds, full_keys) * factor
            h = (first, second)[i]
            dq_ref[:, h * nope : (h + 1) * nope] = grad[:, :nope].astype(BF16)
            turned = grad[:, nope:] if turned is None else turned + grad[:, nope:]
        dqr_ref[:, pair * 2 * rope : (pair + 1) * 2 * rope] = turned.astype(BF16)
        dlat_ref[...] += nn(jnp.concatenate(left, axis=1), jnp.concatenate(right, axis=0))
        zero = jnp.zeros_like(qr)
        qr_split = jnp.concatenate(
            [jnp.where(lane_q < rope, qr, zero), jnp.where(lane_q >= rope, qr, zero)], axis=0
        )
        drope_ref[...] += nn(jnp.concatenate(scores, axis=1), qr_split)


def body(
    query_nope,
    query_rope,
    out_grad,
    latent_codes,
    scale_exponents,
    key_rope,
    block_order,
    up_keys,
    up_values,
):
    tokens, width = latent_codes.shape
    heads, _, nope = up_keys.shape
    rope = key_rope.shape[1]
    group = 4
    factor = 1.0 / math.sqrt(nope + rope)
    scale = jnp.exp2(scale_exponents.astype(F32))
    widened = jnp.repeat(scale, width // scale_exponents.shape[1], axis=1)
    latent = (latent_codes.astype(F32) * widened).astype(BF16)
    place = jnp.broadcast_to(block_order.astype(BF16)[None, :], (tokens, rope))
    pack = jnp.concatenate([latent, key_rope, place], axis=1)
    packs = [pack] + [shifted(pack, "ctx", s) for s in range(1, STEPS)]
    keys = STEPS * tokens
    whole = lambda i: (0, 0)
    cols = lambda i: (0, i)
    per_head = lambda i: (i, 0, 0)
    grad_nope, grad_rope, dlat, drope = pl.pallas_call(
        functools.partial(attend, (tokens, width, nope, rope, group)),
        grid=(heads // group,),
        in_specs=[pl.BlockSpec((tokens, width + 2 * rope), whole)] * STEPS
        + [
            pl.BlockSpec((tokens, group * nope), cols),
            pl.BlockSpec((tokens, group * rope), cols),
            pl.BlockSpec((tokens, group * nope), cols),
            pl.BlockSpec((group, width, nope), per_head),
            pl.BlockSpec((group, width, nope), per_head),
        ],
        out_specs=[
            pl.BlockSpec((tokens, group * nope), cols),
            pl.BlockSpec((tokens, group * rope), cols),
            pl.BlockSpec((keys, width), whole),
            pl.BlockSpec((keys, 2 * rope), whole),
        ],
        out_shape=[
            jax.ShapeDtypeStruct((tokens, heads * nope), BF16),
            jax.ShapeDtypeStruct((tokens, heads * rope), BF16),
            jax.ShapeDtypeStruct((keys, width), F32),
            jax.ShapeDtypeStruct((keys, 2 * rope), F32),
        ],
        scratch_shapes=[
            pltpu.VMEM((keys, width), BF16),
            pltpu.VMEM((keys, 2 * rope), BF16),
            pltpu.VMEM((keys, 2 * rope), BF16),
            pltpu.VMEM((keys, tokens), F32),
        ],
        compiler_params=pltpu.CompilerParams(
            dimension_semantics=("arbitrary",), vmem_limit_bytes=48 * 2**20
        ),
    )(*packs, query_nope, query_rope, out_grad, up_keys, up_values)
    drope = (drope[:, :rope] + drope[:, rope:]) * factor
    both = jnp.concatenate([dlat, drope], axis=1).reshape(STEPS, tokens, width + rope)
    total = both[0]
    for s in range(1, STEPS):
        total = total + shifted(both[s].astype(BF16), "ctx", -s).astype(F32)
    total = lax.psum(total.astype(BF16), "head").astype(F32)
    return (grad_nope, grad_rope, total[:, :width], total[:, width:])


def solution(mesh):
    return jax.shard_map(
        body,
        mesh=mesh,
        in_specs=(
            P("ctx", "head"),
            P("ctx", "head"),
            P("ctx", "head"),
            P("ctx", None),
            P("ctx", None),
            P("ctx", None),
            P("ctx"),
            P("head", None, None),
            P("head", None, None),
        ),
        out_specs=(P("ctx", "head"), P("ctx", "head"), P("ctx", None), P("ctx", None)),
        check_vma=False,
    )
```

profile of v0, /device:TPU:0, one launch (start us, length us, event | category | flops | bytes accessed | tf_op | source)
XLA Modules:
  0.0 138.0 jit_solution(6646183057909618556)
XLA Ops:
  7.2 0.0 all-reduce.2.cloned.1.call-start
  7.9 0.7 multiply_exponential_fusion
  8.5 0.8 copy.14
  9.4 0.1 copy.13
  9.5 0.1 pad.4.clone
  9.6 0.2 broadcast_in_dim.11
  9.8 0.9 fusion.6
  10.8 2.4 %collective-permute-start.2 = (bf16[128,640]{1,0:T(8,128)(2,1)S(1)}, bf16[128,640]{1,0:T(8,128)(2,1)S(1)}, u32[]{:S(2)}, u32[]{:S(2)}) collective-permute-start(bf16[128,640]{1,0:T(8,128)(2,1)S(1)} %maximum_maximum_fusion.pack0), channel_id=1, source_target_pairs={{26,0},{28,2},{30,4},{0,6},{2,8},{4,10},{6,12},{8,14},{10,16},{12,... | collective-permute-start | bytes 491528 | tf_op jit(solution)/shard_map/ppermute | solution.py:19
  13.2 1.5 %collective-permute-start.1 = (bf16[128,640]{1,0:T(8,128)(2,1)S(1)}, bf16[128,640]{1,0:T(8,128)(2,1)S(1)}, u32[]{:S(2)}, u32[]{:S(2)}) collective-permute-start(bf16[128,640]{1,0:T(8,128)(2,1)S(1)} %maximum_maximum_fusion.pack0), channel_id=1, source_target_pairs={{28,0},{30,2},{0,4},{2,6},{4,8},{6,10},{8,12},{10,14},{12,16},{14,... | collective-permute-start | bytes 491528 | tf_op jit(solution)/shard_map/ppermute | solution.py:19
  14.7 0.4 collective-permute-start
  15.2 3.1 %collective-permute-done.2.pack3 = bf16[128,640]{1,0:T(8,128)(2,1)S(1)} collective-permute-done((bf16[128,640]{1,0:T(8,128)(2,1)S(1)}, bf16[128,640]{1,0:T(8,128)(2,1)S(1)}, u32[]{:S(2)}, u32[]{:S(2)}) %collective-permute-start.2) | collective-permute-done | bytes 163872 | tf_op jit(solution)/shard_map/ppermute | solution.py:19
  18.3 7.0 %collective-permute-done.1.pack2 = bf16[128,640]{1,0:T(8,128)(2,1)S(1)} collective-permute-done((bf16[128,640]{1,0:T(8,128)(2,1)S(1)}, bf16[128,640]{1,0:T(8,128)(2,1)S(1)}, u32[]{:S(2)}, u32[]{:S(2)}) %collective-permute-start.1) | collective-permute-done | bytes 163872 | tf_op jit(solution)/shard_map/ppermute | solution.py:19
  25.3 1.5 %collective-permute-done.pack1 = bf16[128,640]{1,0:T(8,128)(2,1)S(1)} collective-permute-done((bf16[128,640]{1,0:T(8,128)(2,1)S(1)}, bf16[128,640]{1,0:T(8,128)(2,1)S(1)}, u32[]{:S(2)}, u32[]{:S(2)}) %collective-permute-start) | collective-permute-done | bytes 163872 | tf_op jit(solution)/shard_map/ppermute | solution.py:19
  26.8 0.0 copy-start
  26.8 1.6 %copy-done = bf16[128,8192]{1,0:T(8,128)(2,1)S(1)} copy-done((bf16[128,8192]{1,0:T(8,128)(2,1)S(1)}, bf16[128,8192]{1,0:T(8,128)(2,1)}, u32[]{:S(2)}) %copy-start) | copy-done | bytes 2097176
  28.3 0.0 copy-start.1
  28.4 1.2 copy-done.1
  29.6 63.6 %shard_map.120 = (bf16[128,8192]{1,0:T(8,128)(2,1)}, bf16[128,4096]{1,0:T(8,128)(2,1)}, f32[512,512]{1,0:T(8,128)S(1)}, f32[512,128]{1,0:T(8,128)S(1)}) custom-call(bf16[128,640]{1,0:T(8,128)(2,1)S(1)} %maximum_maximum_fusion.pack0, bf16[128,640]{1,0:T(8,128)(2,1)S(1)} %collective-permute-done.pack1, bf16[128,640]{1,0:T(8,128)(2,1)S(1)} %collective-permute-done.1.pack2, ...), custom_call_target="tpu_custom_call" | custom-call | tf_op jit(solution)/shard_map/pallas_call | solution.py:149
  93.2 0.1 add_multiply_fusion
  93.3 0.1 fusion
  93.5 0.1 collective-permute-start.3
  93.5 1.9 %collective-permute-start.5 = (bf16[128,576]{1,0:T(8,128)(2,1)S(1)}, bf16[128,576]{1,0:T(8,128)(2,1)S(1)}, u32[]{:S(2)}, u32[]{:S(2)}) collective-permute-start(bf16[128,576]{1,0:T(8,128)(2,1)S(1)} %get-tuple-element.17), channel_id=1, source_target_pairs={{6,0},{8,2},{10,4},{12,6},{14,8},{16,10},{18,12},{20,14},{22,16},{... | collective-permute-start | bytes 442376 | tf_op jit(solution)/shard_map/ppermute | solution.py:19
  95.4 0.0 collective-permute-start.4
  95.4 2.1 %collective-permute-done.3 = bf16[128,576]{1,0:T(8,128)(2,1)S(1)} collective-permute-done((bf16[128,576]{1,0:T(8,128)(2,1)S(1)}, bf16[128,576]{1,0:T(8,128)(2,1)S(1)}, u32[]{:S(2)}, u32[]{:S(2)}) %collective-permute-start.3) | collective-permute-done | bytes 147488 | tf_op jit(solution)/shard_map/ppermute | solution.py:19
  97.5 3.5 %collective-permute-done.5 = bf16[128,576]{1,0:T(8,128)(2,1)S(1)} collective-permute-done((bf16[128,576]{1,0:T(8,128)(2,1)S(1)}, bf16[128,576]{1,0:T(8,128)(2,1)S(1)}, u32[]{:S(2)}, u32[]{:S(2)}) %collective-permute-start.5) | collective-permute-done | bytes 147488 | tf_op jit(solution)/shard_map/ppermute | solution.py:19
  101.1 2.3 %collective-permute-done.4 = bf16[128,576]{1,0:T(8,128)(2,1)S(1)} collective-permute-done((bf16[128,576]{1,0:T(8,128)(2,1)S(1)}, bf16[128,576]{1,0:T(8,128)(2,1)S(1)}, u32[]{:S(2)}, u32[]{:S(2)}) %collective-permute-start.4) | collective-permute-done | bytes 147488 | tf_op jit(solution)/shard_map/ppermute | solution.py:19
  103.4 0.8 fusion.5
  104.1 0.0 all-reduce.2.cloned.1.call-update
  104.2 23.9 %all-reduce.2.cloned.1.call-done = bf16[128,576]{1,0:T(8,128)(2,1)} async-done(((bf16[128,576]{1,0:T(8,128)(2,1)}), bf16[128,576]{1,0:T(8,128)(2,1)}) %all-reduce.2.cloned.1.call-update) | async-done | bytes 147472 | tf_op jit(solution)/shard_map/psum | solution.py:187
  128.1 0.8 slice.45
  128.9 0.7 copy.15
  129.6 1.6 %slice.44 = f32[128,512]{1,0:T(8,128)} slice(bf16[128,576]{1,0:T(8,128)(2,1)} %all-reduce.2.cloned.1.call-done), slice={[0:128], [0:512]} | slice | bytes 524288 | tf_op jit(solution)/shard_map/slice | solution.py:188
  (3 shorter events, 0.1 us)
Async XLA Ops:
  7.2 120.9 %all-reduce.2.cloned.1.call-start = ((), (), s32[]{:S(2)}) async-start(), calls=%async_computation | async-start | bytes 327680 | tf_op jit(solution)/shard_map/psum | solution.py:187
  10.8 7.5 %collective-permute-start.2 = (bf16[128,640]{1,0:T(8,128)(2,1)S(1)}, bf16[128,640]{1,0:T(8,128)(2,1)S(1)}, u32[]{:S(2)}, u32[]{:S(2)}) collective-permute-start(bf16[128,640]{1,0:T(8,128)(2,1)S(1)} %maximum_maximum_fusion.pack0), channel_id=1, source_target_pairs={{26,0},{28,2},{30,4},{0,6},{2,8},{4,10},{6,12},{8,14},{10,16},{12,... | collective-permute-start | bytes 491528 | tf_op jit(solution)/shard_map/ppermute | solution.py:19
  13.2 12.1 %collective-permute-start.1 = (bf16[128,640]{1,0:T(8,128)(2,1)S(1)}, bf16[128,640]{1,0:T(8,128)(2,1)S(1)}, u32[]{:S(2)}, u32[]{:S(2)}) collective-permute-start(bf16[128,640]{1,0:T(8,128)(2,1)S(1)} %maximum_maximum_fusion.pack0), channel_id=1, source_target_pairs={{28,0},{30,2},{0,4},{2,6},{4,8},{6,10},{8,12},{10,14},{12,16},{14,... | collective-permute-start | bytes 491528 | tf_op jit(solution)/shard_map/ppermute | solution.py:19
  14.7 12.0 %collective-permute-start = (bf16[128,640]{1,0:T(8,128)(2,1)S(1)}, bf16[128,640]{1,0:T(8,128)(2,1)S(1)}, u32[]{:S(2)}, u32[]{:S(2)}) collective-permute-start(bf16[128,640]{1,0:T(8,128)(2,1)S(1)} %maximum_maximum_fusion.pack0), channel_id=1, source_target_pairs={{30,0},{0,2},{2,4},{4,6},{6,8},{8,10},{10,12},{12,14},{14,16},{16,... | collective-permute-start | bytes 491528 | tf_op jit(solution)/shard_map/ppermute | solution.py:19
  26.8 1.6 %copy-start = (bf16[128,8192]{1,0:T(8,128)(2,1)S(1)}, bf16[128,8192]{1,0:T(8,128)(2,1)}, u32[]{:S(2)}) copy-start(bf16[128,8192]{1,0:T(8,128)(2,1)} %q_ref.1) | copy-start | bytes 6291460
  28.3 1.2 copy-start.1
  93.5 4.1 %collective-permute-start.3 = (bf16[128,576]{1,0:T(8,128)(2,1)S(1)}, bf16[128,576]{1,0:T(8,128)(2,1)S(1)}, u32[]{:S(2)}, u32[]{:S(2)}) collective-permute-start(bf16[128,576]{1,0:T(8,128)(2,1)S(1)} %get-tuple-element.16), channel_id=1, source_target_pairs={{2,0},{4,2},{6,4},{8,6},{10,8},{12,10},{14,12},{16,14},{18,16},{20... | collective-permute-start | bytes 442376 | tf_op jit(solution)/shard_map/ppermute | solution.py:19
  93.5 7.5 %collective-permute-start.5 = (bf16[128,576]{1,0:T(8,128)(2,1)S(1)}, bf16[128,576]{1,0:T(8,128)(2,1)S(1)}, u32[]{:S(2)}, u32[]{:S(2)}) collective-permute-start(bf16[128,576]{1,0:T(8,128)(2,1)S(1)} %get-tuple-element.17), channel_id=1, source_target_pairs={{6,0},{8,2},{10,4},{12,6},{14,8},{16,10},{18,12},{20,14},{22,16},{... | collective-permute-start | bytes 442376 | tf_op jit(solution)/shard_map/ppermute | solution.py:19
  95.4 8.0 %collective-permute-start.4 = (bf16[128,576]{1,0:T(8,128)(2,1)S(1)}, bf16[128,576]{1,0:T(8,128)(2,1)S(1)}, u32[]{:S(2)}, u32[]{:S(2)}) collective-permute-start(bf16[128,576]{1,0:T(8,128)(2,1)S(1)} %get-tuple-element.18), channel_id=1, source_target_pairs={{4,0},{6,2},{8,4},{10,6},{12,8},{14,10},{16,12},{18,14},{20,16},{2... | collective-permute-start | bytes 442376 | tf_op jit(solution)/shard_map/ppermute | solution.py:19
Sparse Core Ops, SparseCore 0:
  104.3 23.7 all-reduce.1
where the time goes:
time: 138 us
  Pallas kernels  63.6 us (46%)
  waiting for transfers between devices  43.5 us (32%)
  between operations  14.7 us (11%)
  local copies, waits for them, and re-layouts  7.17 us (5%)
  starting transfers between devices  6.39 us (5%)
  other arithmetic  2.64 us (2%)
    pallas_call x1, Pallas kernels, body(): pl.pallas_call(functools.partial(attend, (tokens, width, nope, rope, grou...  63.6 us
    psum x1, waiting for transfers between devices, body(): total = lax.psum(total.astype(BF16), 'head').astype(F32)  23.9 us
    ppermute x6, waiting for transfers between devices, shifted(): return lax.ppermute(block, axis, route)  19.5 us
    ppermute x6, starting transfers between devices, shifted(): return lax.ppermute(block, axis, route)  6.35 us
    unnamed x6, local copies, waits for them, and re-layouts  4.34 us
  transfers between devices with their start and end apart: 7, of which 7 were waited for; matrix products, arithmetic and copies ran while one was open for 0% of the time, Pallas kernels for 0%

commit v1 on v0

--- a/solution.py
+++ b/solution.py
@@ -11,12 +11,7 @@
 STEPS = 4
 F32 = jnp.float32
 BF16 = jnp.bfloat16
-
-
-def shifted(block, axis, distance):
-    devices = range(lax.axis_size(axis))
-    route = [((i - distance) % len(devices), i) for i in devices]
-    return lax.ppermute(block, axis, route)
+MESH = pl.DeviceIdType.MESH
 
 
 def nt(a, b):
@@ -30,13 +25,133 @@
 def tn(a, b):
     return lax.dot_general(a, b, (((0,), (0,)), ((), ())), preferred_element_type=F32)
 
+def wrapped(index, size):
+    return lax.rem(index + size, size)
+
+
+def greet(ring, heads_axis):
+    barrier = pltpu.get_barrier_semaphore()
+    me = lax.axis_index("ctx")
+    count = 0
+    for s in range(1, STEPS):
+        for other in (me + s, me - s):
+            pl.semaphore_signal(
+                barrier, inc=1, device_id={"ctx": wrapped(other, ring)}, device_id_type=MESH
+            )
+            count += 1
+    mine = lax.axis_index("head")
+    for j in range(1, heads_axis):
+        pl.semaphore_signal(
+            barrier,
+            inc=1,
+            device_id={"head": lax.rem(mine + j, heads_axis)},
+            device_id_type=MESH,
+        )
+        count += 1
+    pl.semaphore_wait(barrier, count)
+
+
+def collect(ring, codes_ref, exps_ref, rope_ref, order_ref, out, send_sem, recv_sem):
+    tokens, width = codes_ref.shape
+    rope = rope_ref.shape[1]
+    groups = exps_ref.shape[1]
+    part = width // groups
+    exps = exps_ref[...]
+    scale = jnp.where(
+        exps == -2, 0.25, jnp.where(exps == -1, 0.5, jnp.where(exps == 0, 1.0, 2.0))
+    ).astype(F32)
+    for j in range(groups):
+        span = slice(j * part, (j + 1) * part)
+        out[0, :, span] = (codes_ref[:, span].astype(F32) * scale[:, j : j + 1]).astype(BF16)
+    place = jnp.full((tokens, rope), order_ref[0], jnp.int32).astype(F32)
+    out[0, :, width:] = jnp.concatenate([rope_ref[...].astype(F32), place], axis=1).astype(BF16)
+    greet(ring, 1)
+    me = lax.axis_index("ctx")
+    copies = []
+    for s in (3, 2, 1):
+        copy = pltpu.make_async_remote_copy(
+            src_ref=out.at[0],
+            dst_ref=out.at[s],
+            send_sem=send_sem.at[s],
+            recv_sem=recv_sem.at[s],
+            device_id={"ctx": wrapped(me + s, ring)},
+            device_id_type=MESH,
+        )
+        copy.start()
+        copies.append(copy)
+    for copy in copies:
+        copy.wait()
+
+
+def bring_home(
+    sizes,
+    dlat_ref,
+    drope_ref,
+    latent_out,
+    rope_out,
+    parts,
+    landed,
+    summed,
+    send_sem,
+    recv_sem,
+    head_send,
+    head_recv,
+):
+    ring, heads_axis, factor = sizes
+    tokens, width = latent_out.shape
+    rope = rope_out.shape[1]
+    me = lax.axis_index("ctx")
+    mine = lax.axis_index("head")
+    for s in range(1, STEPS):
+        rows = pl.ds(s * tokens, tokens)
+        parts[s, :, :width] = dlat_ref[rows, :].astype(BF16)
+        parts[s, :, width:] = drope_ref[rows, :].astype(BF16)
+    greet(ring, heads_axis)
+    copies = []
+    for s in (3, 2, 1):
+        copy = pltpu.make_async_remote_copy(
+            src_ref=parts.at[s],
+            dst_ref=landed.at[s],
+            send_sem=send_sem.at[s],
+            recv_sem=recv_sem.at[s],
+            device_id={"ctx": wrapped(me - s, ring)},
+            device_id_type=MESH,
+        )
+        copy.start()
+        copies.append(copy)
+    for copy in copies:
+        copy.wait()
+    lat_total = dlat_ref[:tokens, :]
+    rope_total = drope_ref[:tokens, :]
+    for s in range(1, STEPS):
+        lat_total = lat_total + landed[s, :, :width].astype(F32)
+        rope_total = rope_total + landed[s, :, width:].astype(F32)
+    summed[mine, :, :width] = lat_total.astype(BF16)
+    summed[mine, :, width:] = rope_total.astype(BF16)
+    copies = []
+    for j in range(1, heads_axis):
+        copy = pltpu.make_async_remote_copy(
+            src_ref=summed.at[mine],
+            dst_ref=summed.at[mine],
+            send_sem=head_send.at[j],
+            recv_sem=head_recv.at[j],
+            device_id={"head": lax.rem(mine + j, heads_axis)},
+            device_id_type=MESH,
+        )
+        copy.start()
+        copies.append(copy)
+    for copy in copies:
+        copy.wait()
+    total = summed[0].astype(F32)
+    for j in range(1, heads_axis):
+        total = total + summed[j].astype(F32)
+    latent_out[...] = total[:, :width]
+    rope_out[...] = (total[:, width : width + rope] + total[:, width + rope :]) * factor
+
 
 def attend(
     dims,
-    pack0,
-    pack1,
-    pack2,
-    pack3,
+    packs,
     q_ref,
     qr_ref,
     g_ref,
@@ -62,10 +177,10 @@
         row = lax.broadcasted_iota(jnp.int32, (tokens, tokens), 0).astype(F32)
         col = lax.broadcasted_iota(jnp.int32, (tokens, tokens), 1).astype(F32)
         own = None
-        for s, pack in enumerate((pack0, pack1, pack2, pack3)):
+        for s in range(STEPS):
             rows = pl.ds(s * tokens, tokens)
-            lat[rows, :] = pack[:, :width]
-            tail = pack[:, width:].astype(F32)
+            lat[rows, :] = packs[s, :, :width]
+            tail = packs[s, :, width:].astype(F32)
             turned = pltpu.roll(tail, rope, 1)
             rope_even[rows, :] = jnp.where(lane < rope, tail, 0.0).astype(BF16)
             rope_odd[rows, :] = jnp.where(lane >= rope, turned, 0.0).astype(BF16)
@@ -136,12 +251,17 @@
     rope = key_rope.shape[1]
     group = 4
     factor = 1.0 / math.sqrt(nope + rope)
-    scale = jnp.exp2(scale_exponents.astype(F32))
-    widened = jnp.repeat(scale, width // scale_exponents.shape[1], axis=1)
-    latent = (latent_codes.astype(F32) * widened).astype(BF16)
-    place = jnp.broadcast_to(block_order.astype(BF16)[None, :], (tokens, rope))
-    pack = jnp.concatenate([latent, key_rope, place], axis=1)
-    packs = [pack] + [shifted(pack, "ctx", s) for s in range(1, STEPS)]
+    ring = lax.axis_size("ctx")
+    heads_axis = lax.axis_size("head")
+    vmem = pl.BlockSpec(memory_space=pltpu.VMEM)
+    packs = pl.pallas_call(
+        functools.partial(collect, ring),
+        out_shape=jax.ShapeDtypeStruct((STEPS, tokens, width + 2 * rope), BF16),
+        in_specs=[vmem] * 3 + [pl.BlockSpec(memory_space=pltpu.SMEM)],
+        out_specs=vmem,
+        scratch_shapes=[pltpu.SemaphoreType.DMA((STEPS,)), pltpu.SemaphoreType.DMA((STEPS,))],
+        compiler_params=pltpu.CompilerParams(collective_id=0, has_side_effects=True),
+    )(latent_codes, scale_exponents, key_rope, block_order)
     keys = STEPS * tokens
     whole = lambda i: (0, 0)
     cols = lambda i: (0, i)
@@ -149,7 +269,7 @@
     grad_nope, grad_rope, dlat, drope = pl.pallas_call(
         functools.partial(attend, (tokens, width, nope, rope, group)),
         grid=(heads // group,),
-        in_specs=[pl.BlockSpec((tokens, width + 2 * rope), whole)] * STEPS
+        in_specs=[pl.BlockSpec((STEPS, tokens, width + 2 * rope), lambda i: (0, 0, 0))]
         + [
             pl.BlockSpec((tokens, group * nope), cols),
             pl.BlockSpec((tokens, group * rope), cols),
@@ -178,14 +298,30 @@
         compiler_params=pltpu.CompilerParams(
             dimension_semantics=("arbitrary",), vmem_limit_bytes=48 * 2**20
         ),
-    )(*packs, query_nope, query_rope, out_grad, up_keys, up_values)
-    drope = (drope[:, :rope] + drope[:, rope:]) * factor
-    both = jnp.concatenate([dlat, drope], axis=1).reshape(STEPS, tokens, width + rope)
-    total = both[0]
-    for s in range(1, STEPS):
-        total = total + shifted(both[s].astype(BF16), "ctx", -s).astype(F32)
-    total = lax.psum(total.astype(BF16), "head").astype(F32)
-    return (grad_nope, grad_rope, total[:, :width], total[:, width:])
+    )(packs, query_nope, query_rope, out_grad, up_keys, up_values)
+    block = (tokens, width + 2 * rope)
+    grad_latent, grad_rope_keys = pl.pallas_call(
+        functools.partial(bring_home, (ring, heads_axis, factor)),
+        out_shape=[
+            jax.ShapeDtypeStruct((tokens, width), F32),
+            jax.ShapeDtypeStruct((tokens, rope), F32),
+        ],
+        in_specs=[vmem, vmem],
+        out_specs=[vmem, vmem],
+        scratch_shapes=[
+            pltpu.VMEM((STEPS,) + block, BF16),
+            pltpu.VMEM((STEPS,) + block, BF16),
+            pltpu.VMEM((heads_axis,) + block, BF16),
+            pltpu.SemaphoreType.DMA((STEPS,)),
+            pltpu.SemaphoreType.DMA((STEPS,)),
+            pltpu.SemaphoreType.DMA((heads_axis,)),
+            pltpu.SemaphoreType.DMA((heads_axis,)),
+        ],
+        compiler_params=pltpu.CompilerParams(
+            collective_id=1, has_side_effects=True, vmem_limit_bytes=16 * 2**20
+        ),
+    )(dlat, drope)
+    return (grad_nope, grad_rope, grad_latent, grad_rope_keys)
 
 
 def solution(mesh):

time: 138 us -> 108 us (0.78)
  waiting for transfers between devices: 43.5 us -> 0 us
  Pallas kernels: 63.6 us -> 98 us
  between operations: 14.7 us -> 1.31 us
  starting transfers between devices: 6.39 us -> 0 us
  other arithmetic: 2.64 us -> 0 us
    pallas_call x0 -> x2, Pallas kernels: none -> 34.4 us  [the longest x1 18.3 us: body(): pl.pallas_call(functools.partial(collect, ring), out_shape=jax.ShapeDtype...]
    psum x1 -> x0, waiting for transfers between devices: 23.9 us -> none  [body(): total = lax.psum(total.astype(BF16), 'head').astype(F32)]
    ppermute x6 -> x0, waiting for transfers between devices: 19.5 us -> none  [shifted(): return lax.ppermute(block, axis, route)]
    ppermute x6 -> x0, starting transfers between devices: 6.35 us -> none  [shifted(): return lax.ppermute(block, axis, route)]
    unnamed x6 -> x10, local copies, waits for them, and re-layouts: 4.34 us -> 8.15 us
    slice x3 -> x0, local copies, waits for them, and re-layouts: 2.44 us -> none  [the longest x2 2.39 us: body(): return (grad_nope, grad_rope, total[:, :width], total[:, width:])]
    convert_element_type x2 -> x0, other arithmetic: 1.69 us -> none  [the longest x1 0.94 us: body(): latent = (latent_codes.astype(F32) * widened).astype(BF16)]
  transfers between devices with their start and end apart: 7 -> 0, of which waited for: 7 -> 0; matrix products, arithmetic and copies ran while one was open for 0% -> 0% of each run, Pallas kernels for 0% -> 0%
where the time goes in v1:
time: 108 us; the launch traced here: 107 us
  Pallas kernels  98 us (91%)
  local copies, waits for them, and re-layouts  8.15 us (8%)
  between operations  1.31 us (1%)
    pallas_call x1, Pallas kernels, body(): pl.pallas_call(functools.partial(attend, (tokens, width, nope, rope, grou...  63.6 us
    pallas_call x1, Pallas kernels, body(): pl.pallas_call(functools.partial(collect, ring), out_shape=jax.ShapeDtype...  18.3 us
    pallas_call x1, Pallas kernels, body(): pl.pallas_call(functools.partial(bring_home, (ring, heads_axis, factor)),...  16.1 us
    unnamed x10, local copies, waits for them, and re-layouts  8.15 us

profile of v1, /device:TPU:0, one launch (start us, length us, event | category | flops | bytes accessed | tf_op | source)
XLA Modules:
  0.0 107.4 jit_solution(12949909826255216023)
XLA Ops:
  1.3 1.4 %copy.14.rope_ref = bf16[128,64]{1,0:T(8,128)(2,1)} copy(bf16[128,64]{0,1:T(8,128)(2,1)} %param.14) | data formatting | bytes 32768 | tf_op args[5]
  2.7 1.4 %copy.13.exps_ref = s32[128,4]{1,0:T(8,128)} copy(s32[128,4]{0,1:T(4,128)} %param.13) | data formatting | bytes 4096 | tf_op args[4]
  4.1 18.3 %shard_map.120.packs = bf16[4,128,640]{2,1,0:T(8,128)(2,1)} custom-call(bf16[128,512]{1,0:T(8,128)(2,1)} %codes_ref.1, s32[128,4]{1,0:T(8,128)} %copy.13.exps_ref, bf16[128,64]{1,0:T(8,128)(2,1)} %copy.14.rope_ref, s32[1]{0:T(128)S(6)} %copy.17.order_ref), custom_call_target="tpu_custom_call" | custom-call | tf_op jit(solution)/shard_map/pallas_call | solution.py:257
  22.4 0.0 copy-start
  22.4 1.1 %copy-done = bf16[4,128,640]{2,1,0:T(8,128)(2,1)S(1)} copy-done((bf16[4,128,640]{2,1,0:T(8,128)(2,1)S(1)}, bf16[4,128,640]{2,1,0:T(8,128)(2,1)}, u32[]{:S(2)}) %copy-start) | copy-done | bytes 655384
  23.5 0.0 copy-start.1
  23.5 1.6 %copy-done.1 = bf16[128,8192]{1,0:T(8,128)(2,1)S(1)} copy-done((bf16[128,8192]{1,0:T(8,128)(2,1)S(1)}, bf16[128,8192]{1,0:T(8,128)(2,1)}, u32[]{:S(2)}) %copy-start.1) | copy-done | bytes 2097176
  25.1 0.0 copy-start.2
  25.1 1.2 %copy-done.2 = bf16[128,4096]{1,0:T(8,128)(2,1)S(1)} copy-done((bf16[128,4096]{1,0:T(8,128)(2,1)S(1)}, bf16[128,4096]{1,0:T(8,128)(2,1)}, u32[]{:S(2)}) %copy-start.2) | copy-done | bytes 1048600
  26.3 63.6 %shard_map.121 = (bf16[128,8192]{1,0:T(8,128)(2,1)}, bf16[128,4096]{1,0:T(8,128)(2,1)}, f32[512,512]{1,0:T(8,128)S(1)}, f32[512,128]{1,0:T(8,128)S(1)}) custom-call(bf16[4,128,640]{2,1,0:T(8,128)(2,1)S(1)} %copy-done, bf16[128,8192]{1,0:T(8,128)(2,1)S(1)} %copy-done.1, bf16[128,4096]{1,0:T(8,128)(2,1)S(1)} %copy-done.2, bf16[128,8192]{1,0:T(8,128)(2,1)} %g_ref.1, ...), custom_call_target="tpu_custom_call" | custom-call | tf_op jit(solution)/shard_map/pallas_call | solution.py:269
  89.9 16.1 %shard_map.122 = (f32[128,512]{1,0:T(8,128)S(1)}, f32[128,64]{1,0:T(8,128)S(1)}) custom-call(f32[512,512]{1,0:T(8,128)S(1)} %get-tuple-element.12.dlat_ref, f32[512,128]{1,0:T(8,128)S(1)} %get-tuple-element.13.drope_ref), custom_call_target="tpu_custom_call" | custom-call | tf_op jit(solution)/shard_map/pallas_call | solution.py:303
  106.0 0.7 copy.15
  106.7 0.7 copy.18
Async XLA Ops:
  22.4 1.1 %copy-start = (bf16[4,128,640]{2,1,0:T(8,128)(2,1)S(1)}, bf16[4,128,640]{2,1,0:T(8,128)(2,1)}, u32[]{:S(2)}) copy-start(bf16[4,128,640]{2,1,0:T(8,128)(2,1)} %shard_map.120.packs) | copy-start | bytes 1966084
  23.5 1.6 %copy-start.1 = (bf16[128,8192]{1,0:T(8,128)(2,1)S(1)}, bf16[128,8192]{1,0:T(8,128)(2,1)}, u32[]{:S(2)}) copy-start(bf16[128,8192]{1,0:T(8,128)(2,1)} %q_ref.1) | copy-start | bytes 6291460
  25.1 1.2 %copy-start.2 = (bf16[128,4096]{1,0:T(8,128)(2,1)S(1)}, bf16[128,4096]{1,0:T(8,128)(2,1)}, u32[]{:S(2)}) copy-start(bf16[128,4096]{1,0:T(8,128)(2,1)} %qr_ref.1) | copy-start | bytes 3145732

commit v2 on v1

--- a/solution.py
+++ b/solution.py
@@ -48,24 +48,26 @@
             device_id_type=MESH,
         )
         count += 1
-    pl.semaphore_wait(barrier, count)
+    return lambda: pl.semaphore_wait(barrier, count)
 
 
 def collect(ring, codes_ref, exps_ref, rope_ref, order_ref, out, send_sem, recv_sem):
+    met = greet(ring, 1)
     tokens, width = codes_ref.shape
-    rope = rope_ref.shape[1]
-    groups = exps_ref.shape[1]
+    rope = rope_ref.shape[0]
+    groups = exps_ref.shape[0]
     part = width // groups
     exps = exps_ref[...]
     scale = jnp.where(
         exps == -2, 0.25, jnp.where(exps == -1, 0.5, jnp.where(exps == 0, 1.0, 2.0))
     ).astype(F32)
+    scale = jnp.concatenate([scale, jnp.zeros((8 - groups, tokens), F32)], axis=0).T
     for j in range(groups):
         span = slice(j * part, (j + 1) * part)
         out[0, :, span] = (codes_ref[:, span].astype(F32) * scale[:, j : j + 1]).astype(BF16)
     place = jnp.full((tokens, rope), order_ref[0], jnp.int32).astype(F32)
-    out[0, :, width:] = jnp.concatenate([rope_ref[...].astype(F32), place], axis=1).astype(BF16)
-    greet(ring, 1)
+    out[0, :, width:] = jnp.concatenate([rope_ref[...].astype(F32).T, place], axis=1).astype(BF16)
+    met()
     me = lax.axis_index("ctx")
     copies = []
     for s in (3, 2, 1):
@@ -98,15 +100,16 @@
     head_recv,
 ):
     ring, heads_axis, factor = sizes
+    met = greet(ring, heads_axis)
     tokens, width = latent_out.shape
-    rope = rope_out.shape[1]
+    rope = rope_out.shape[0]
     me = lax.axis_index("ctx")
     mine = lax.axis_index("head")
     for s in range(1, STEPS):
         rows = pl.ds(s * tokens, tokens)
         parts[s, :, :width] = dlat_ref[rows, :].astype(BF16)
         parts[s, :, width:] = drope_ref[rows, :].astype(BF16)
-    greet(ring, heads_axis)
+    met()
     copies = []
     for s in (3, 2, 1):
         copy = pltpu.make_async_remote_copy(
@@ -146,7 +149,8 @@
     for j in range(1, heads_axis):
         total = total + summed[j].astype(F32)
     latent_out[...] = total[:, :width]
-    rope_out[...] = (total[:, width : width + rope] + total[:, width + rope :]) * factor
+    tail = total[:, width:].T
+    rope_out[...] = (tail[:rope] + tail[rope:]) * factor
 
 
 def attend(
@@ -199,9 +203,9 @@
         keys = nn(latent, jnp.concatenate([uk_ref[first], uk_ref[second]], axis=1)).astype(BF16)
         q = [q_ref[:, h * nope : (h + 1) * nope] for h in (first, second)]
         g = [g_ref[:, h * nope : (h + 1) * nope] for h in (first, second)]
-        q_lat = [(nt(q[i], uk_ref[h]) * factor).astype(BF16) for i, h in enumerate((first, second))]
-        g_lat = [nt(g[i], uv_ref[h]).astype(BF16) for i, h in enumerate((first, second))]
-        dp_both = nt(latent, jnp.concatenate(g_lat, axis=0))
+        q_lat = [(nt(uk_ref[h], q[i]) * factor).astype(BF16) for i, h in enumerate((first, second))]
+        g_lat = [nt(uv_ref[h], g[i]).astype(BF16) for i, h in enumerate((first, second))]
+        dp_both = nn(latent, jnp.concatenate(g_lat, axis=1))
         left = []
         right = []
         turned = None
@@ -222,12 +226,12 @@
             scores.append(ds)
             left += [ds, prob.astype(BF16)]
             right += [q_lat[i], g_lat[i]]
-            grad = tn(ds, full_keys) * factor
+            grad = tn(full_keys, ds).T * factor
             h = (first, second)[i]
             dq_ref[:, h * nope : (h + 1) * nope] = grad[:, :nope].astype(BF16)
             turned = grad[:, nope:] if turned is None else turned + grad[:, nope:]
         dqr_ref[:, pair * 2 * rope : (pair + 1) * 2 * rope] = turned.astype(BF16)
-        dlat_ref[...] += nn(jnp.concatenate(left, axis=1), jnp.concatenate(right, axis=0))
+        dlat_ref[...] += nt(jnp.concatenate(left, axis=1), jnp.concatenate(right, axis=1))
         zero = jnp.zeros_like(qr)
         qr_split = jnp.concatenate(
             [jnp.where(lane_q < rope, qr, zero), jnp.where(lane_q >= rope, qr, zero)], axis=0
@@ -249,7 +253,7 @@
     tokens, width = latent_codes.shape
     heads, _, nope = up_keys.shape
     rope = key_rope.shape[1]
-    group = 4
+    group = 8
     factor = 1.0 / math.sqrt(nope + rope)
     ring = lax.axis_size("ctx")
     heads_axis = lax.axis_size("head")
@@ -261,7 +265,7 @@
         out_specs=vmem,
         scratch_shapes=[pltpu.SemaphoreType.DMA((STEPS,)), pltpu.SemaphoreType.DMA((STEPS,))],
         compiler_params=pltpu.CompilerParams(collective_id=0, has_side_effects=True),
-    )(latent_codes, scale_exponents, key_rope, block_order)
+    )(latent_codes, scale_exponents.T, key_rope.T, block_order)
     keys = STEPS * tokens
     whole = lambda i: (0, 0)
     cols = lambda i: (0, i)
@@ -296,7 +300,7 @@
             pltpu.VMEM((keys, tokens), F32),
         ],
         compiler_params=pltpu.CompilerParams(
-            dimension_semantics=("arbitrary",), vmem_limit_bytes=48 * 2**20
+            dimension_semantics=("arbitrary",), vmem_limit_bytes=60 * 2**20
         ),
     )(packs, query_nope, query_rope, out_grad, up_keys, up_values)
     block = (tokens, width + 2 * rope)
@@ -304,7 +308,7 @@
         functools.partial(bring_home, (ring, heads_axis, factor)),
         out_shape=[
             jax.ShapeDtypeStruct((tokens, width), F32),
-            jax.ShapeDtypeStruct((tokens, rope), F32),
+            jax.ShapeDtypeStruct((rope, tokens), F32),
         ],
         in_specs=[vmem, vmem],
         out_specs=[vmem, vmem],
@@ -321,7 +325,7 @@
             collective_id=1, has_side_effects=True, vmem_limit_bytes=16 * 2**20
         ),
     )(dlat, drope)
-    return (grad_nope, grad_rope, grad_latent, grad_rope_keys)
+    return (grad_nope, grad_rope, grad_latent, grad_rope_keys.T)
 
 
 def solution(mesh):

time: 108 us -> 93.4 us (0.86)
  Pallas kernels: 98 us -> 88.4 us
  local copies, waits for them, and re-layouts: 8.15 us -> 3.49 us
    pallas_call x1, Pallas kernels: 63.6 us -> 54.2 us  [body(): pl.pallas_call(functools.partial(attend, (tokens, width, nope, rope, grou...]
    unnamed x10 -> x6, local copies, waits for them, and re-layouts: 8.15 us -> 3.49 us
where the time goes in v2:
time: 93.4 us; the launch traced here: 93.2 us
  Pallas kernels  88.4 us (95%)
  local copies, waits for them, and re-layouts  3.49 us (4%)
  between operations  1.31 us (1%)
    pallas_call x1, Pallas kernels, body(): pl.pallas_call(functools.partial(attend, (tokens, width, nope, rope, grou...  54.2 us
    pallas_call x1, Pallas kernels, body(): pl.pallas_call(functools.partial(collect, ring), out_shape=jax.ShapeDtype...  18.2 us
    pallas_call x1, Pallas kernels, body(): pl.pallas_call(functools.partial(bring_home, (ring, heads_axis, factor)),...  16.1 us
    unnamed x6, local copies, waits for them, and re-layouts  3.49 us

profile of v2, /device:TPU:0, one launch (start us, length us, event | category | flops | bytes accessed | tf_op | source)
XLA Modules:
  0.0 93.2 jit_solution(13200378091192223930)
XLA Ops:
  1.3 18.2 %shard_map.120.packs = bf16[4,128,640]{2,1,0:T(8,128)(2,1)} custom-call(bf16[128,512]{1,0:T(8,128)(2,1)} %codes_ref.1, s32[4,128]{1,0:T(4,128)} %bitcast.5, bf16[64,128]{1,0:T(8,128)(2,1)} %bitcast.4, s32[1]{0:T(128)S(6)} %copy.15.order_ref), custom_call_target="tpu_custom_call" | custom-call | tf_op jit(solution)/shard_map/pallas_call | solution.py:261
  19.5 54.2 %shard_map.121 = (bf16[128,8192]{1,0:T(8,128)(2,1)}, bf16[128,4096]{1,0:T(8,128)(2,1)}, f32[512,512]{1,0:T(8,128)}, f32[512,128]{1,0:T(8,128)}) custom-call(bf16[4,128,640]{2,1,0:T(8,128)(2,1)} %shard_map.120.packs, bf16[128,8192]{1,0:T(8,128)(2,1)} %q_ref.1, bf16[128,4096]{1,0:T(8,128)(2,1)} %qr_ref.1, bf16[128,8192]{1,0:T(8,128)(2,1)} %g_ref.1, ...), custom_call_target="tpu_custom_call" | custom-call | tf_op jit(solution)/shard_map/pallas_call | solution.py:273
  73.7 0.0 copy-start
  73.7 1.2 %copy-done = f32[512,512]{1,0:T(8,128)S(1)} copy-done((f32[512,512]{1,0:T(8,128)S(1)}, f32[512,512]{1,0:T(8,128)}, u32[]{:S(2)}) %copy-start) | copy-done | bytes 1048600
  74.9 0.0 copy-start.1
  74.9 0.9 %copy-done.1 = f32[512,128]{1,0:T(8,128)S(1)} copy-done((f32[512,128]{1,0:T(8,128)S(1)}, f32[512,128]{1,0:T(8,128)}, u32[]{:S(2)}) %copy-start.1) | copy-done | bytes 262168
  75.8 16.1 %shard_map.122 = (f32[128,512]{1,0:T(8,128)S(1)}, f32[64,128]{1,0:T(8,128)S(1)}) custom-call(f32[512,512]{1,0:T(8,128)S(1)} %copy-done, f32[512,128]{1,0:T(8,128)S(1)} %copy-done.1), custom_call_target="tpu_custom_call" | custom-call | tf_op jit(solution)/shard_map/pallas_call | solution.py:307
  91.9 0.7 copy.16
  92.6 0.6 copy.17
Async XLA Ops:
  73.7 1.2 %copy-start = (f32[512,512]{1,0:T(8,128)S(1)}, f32[512,512]{1,0:T(8,128)}, u32[]{:S(2)}) copy-start(f32[512,512]{1,0:T(8,128)} %get-tuple-element.12.dlat_ref) | copy-start | bytes 3145732
  74.9 0.9 %copy-start.1 = (f32[512,128]{1,0:T(8,128)S(1)}, f32[512,128]{1,0:T(8,128)}, u32[]{:S(2)}) copy-start(f32[512,128]{1,0:T(8,128)} %get-tuple-element.13.drope_ref) | copy-start | bytes 786436

commit v3 on v2

--- a/solution.py
+++ b/solution.py
@@ -110,40 +110,43 @@
         parts[s, :, :width] = dlat_ref[rows, :].astype(BF16)
         parts[s, :, width:] = drope_ref[rows, :].astype(BF16)
     met()
+    spans = [pl.ds(k * (tokens // 2), tokens // 2) for k in range(2)]
     copies = []
-    for s in (3, 2, 1):
-        copy = pltpu.make_async_remote_copy(
-            src_ref=parts.at[s],
-            dst_ref=landed.at[s],
-            send_sem=send_sem.at[s],
-            recv_sem=recv_sem.at[s],
-            device_id={"ctx": wrapped(me - s, ring)},
-            device_id_type=MESH,
-        )
-        copy.start()
-        copies.append(copy)
-    for copy in copies:
-        copy.wait()
-    lat_total = dlat_ref[:tokens, :]
-    rope_total = drope_ref[:tokens, :]
-    for s in range(1, STEPS):
-        lat_total = lat_total + landed[s, :, :width].astype(F32)
-        rope_total = rope_total + landed[s, :, width:].astype(F32)
-    summed[mine, :, :width] = lat_total.astype(BF16)
-    summed[mine, :, width:] = rope_total.astype(BF16)
-    copies = []
-    for j in range(1, heads_axis):
-        copy = pltpu.make_async_remote_copy(
-            src_ref=summed.at[mine],
-            dst_ref=summed.at[mine],
-            send_sem=head_send.at[j],
-            recv_sem=head_recv.at[j],
-            device_id={"head": lax.rem(mine + j, heads_axis)},
-            device_id_type=MESH,
-        )
-        copy.start()
-        copies.append(copy)
-    for copy in copies:
+    for k, span in enumerate(spans):
+        for s in (3, 2, 1):
+            copy = pltpu.make_async_remote_copy(
+                src_ref=parts.at[s, span],
+                dst_ref=landed.at[s, span],
+                send_sem=send_sem.at[k, s],
+                recv_sem=recv_sem.at[k, s],
+                device_id={"ctx": wrapped(me - s, ring)},
+                device_id_type=MESH,
+            )
+            copy.start()
+            copies.append(copy)
+    exchanges = []
+    for k, span in enumerate(spans):
+        for copy in copies[k * (STEPS - 1) : (k + 1) * (STEPS - 1)]:
+            copy.wait()
+        lat_total = dlat_ref[span, :]
+        rope_total = drope_ref[span, :]
+        for s in range(1, STEPS):
+            lat_total = lat_total + landed[s, span, :width].astype(F32)
+            rope_total = rope_total + landed[s, span, width:].astype(F32)
+        summed[mine, span, :width] = lat_total.astype(BF16)
+        summed[mine, span, width:] = rope_total.astype(BF16)
+        for j in range(1, heads_axis):
+            copy = pltpu.make_async_remote_copy(
+                src_ref=summed.at[mine, span],
+                dst_ref=summed.at[mine, span],
+                send_sem=head_send.at[k, j],
+                recv_sem=head_recv.at[k, j],
+                device_id={"head": lax.rem(mine + j, heads_axis)},
+                device_id_type=MESH,
+            )
+            copy.start()
+            exchanges.append(copy)
+    for copy in exchanges:
         copy.wait()
     total = summed[0].astype(F32)
     for j in range(1, heads_axis):
@@ -316,10 +319,10 @@
             pltpu.VMEM((STEPS,) + block, BF16),
             pltpu.VMEM((STEPS,) + block, BF16),
             pltpu.VMEM((heads_axis,) + block, BF16),
-            pltpu.SemaphoreType.DMA((STEPS,)),
-            pltpu.SemaphoreType.DMA((STEPS,)),
-            pltpu.SemaphoreType.DMA((heads_axis,)),
-            pltpu.SemaphoreType.DMA((heads_axis,)),
+            pltpu.SemaphoreType.DMA((2, STEPS)),
+            pltpu.SemaphoreType.DMA((2, STEPS)),
+            pltpu.SemaphoreType.DMA((2, heads_axis)),
+            pltpu.SemaphoreType.DMA((2, heads_axis)),
         ],
         compiler_params=pltpu.CompilerParams(
             collective_id=1, has_side_effects=True, vmem_limit_bytes=16 * 2**20

time: 93.4 us -> 92.1 us (0.986)
  Pallas kernels: 88.4 us -> 87 us
    pallas_call x1, Pallas kernels: 16.1 us -> 14.7 us  [body(): pl.pallas_call(functools.partial(bring_home, (ring, heads_axis, factor)),...]
where the time goes in v3:
time: 92.1 us; the launch traced here: 91.8 us
  Pallas kernels  87 us (94%)
  local copies, waits for them, and re-layouts  3.49 us (4%)
  between operations  1.31 us (1%)
    pallas_call x1, Pallas kernels, body(): pl.pallas_call(functools.partial(attend, (tokens, width, nope, rope, grou...  54.2 us
    pallas_call x1, Pallas kernels, body(): pl.pallas_call(functools.partial(collect, ring), out_shape=jax.ShapeDtype...  18.2 us
    pallas_call x1, Pallas kernels, body(): pl.pallas_call(functools.partial(bring_home, (ring, heads_axis, factor)),...  14.7 us
    unnamed x6, local copies, waits for them, and re-layouts  3.49 us

profile of v3, /device:TPU:0, one launch (start us, length us, event | category | flops | bytes accessed | tf_op | source)
XLA Modules:
  0.0 91.8 jit_solution(9046254740451443953)
XLA Ops:
  1.3 18.2 %shard_map.120.packs = bf16[4,128,640]{2,1,0:T(8,128)(2,1)} custom-call(bf16[128,512]{1,0:T(8,128)(2,1)} %codes_ref.1, s32[4,128]{1,0:T(4,128)} %bitcast.5, bf16[64,128]{1,0:T(8,128)(2,1)} %bitcast.4, s32[1]{0:T(128)S(6)} %copy.15.order_ref), custom_call_target="tpu_custom_call" | custom-call | tf_op jit(solution)/shard_map/pallas_call | solution.py:264
  19.5 54.2 %shard_map.121 = (bf16[128,8192]{1,0:T(8,128)(2,1)}, bf16[128,4096]{1,0:T(8,128)(2,1)}, f32[512,512]{1,0:T(8,128)}, f32[512,128]{1,0:T(8,128)}) custom-call(bf16[4,128,640]{2,1,0:T(8,128)(2,1)} %shard_map.120.packs, bf16[128,8192]{1,0:T(8,128)(2,1)} %q_ref.1, bf16[128,4096]{1,0:T(8,128)(2,1)} %qr_ref.1, bf16[128,8192]{1,0:T(8,128)(2,1)} %g_ref.1, ...), custom_call_target="tpu_custom_call" | custom-call | tf_op jit(solution)/shard_map/pallas_call | solution.py:276
  73.7 0.0 copy-start
  73.7 1.2 %copy-done = f32[512,512]{1,0:T(8,128)S(1)} copy-done((f32[512,512]{1,0:T(8,128)S(1)}, f32[512,512]{1,0:T(8,128)}, u32[]{:S(2)}) %copy-start) | copy-done | bytes 1048600
  74.9 0.0 copy-start.1
  74.9 0.9 %copy-done.1 = f32[512,128]{1,0:T(8,128)S(1)} copy-done((f32[512,128]{1,0:T(8,128)S(1)}, f32[512,128]{1,0:T(8,128)}, u32[]{:S(2)}) %copy-start.1) | copy-done | bytes 262168
  75.8 14.7 %shard_map.122 = (f32[128,512]{1,0:T(8,128)S(1)}, f32[64,128]{1,0:T(8,128)S(1)}) custom-call(f32[512,512]{1,0:T(8,128)S(1)} %copy-done, f32[512,128]{1,0:T(8,128)S(1)} %copy-done.1), custom_call_target="tpu_custom_call" | custom-call | tf_op jit(solution)/shard_map/pallas_call | solution.py:310
  90.5 0.7 copy.16
  91.2 0.6 copy.17
Async XLA Ops:
  73.7 1.2 %copy-start = (f32[512,512]{1,0:T(8,128)S(1)}, f32[512,512]{1,0:T(8,128)}, u32[]{:S(2)}) copy-start(f32[512,512]{1,0:T(8,128)} %get-tuple-element.12.dlat_ref) | copy-start | bytes 3145732
  74.9 0.9 %copy-start.1 = (f32[512,128]{1,0:T(8,128)S(1)}, f32[512,128]{1,0:T(8,128)}, u32[]{:S(2)}) copy-start(f32[512,128]{1,0:T(8,128)} %get-tuple-element.13.drope_ref) | copy-start | bytes 786436
